TPU v7x, 512 devices: a whole 4x4x16 slice. The times are simulated.
512 devices in a mesh: freq: 2 (over x_hi), grp: 16 (over z), sub: 16 (over y, x_lo, core).
Axes of the slice: x: 4 (x_hi: 2, x_lo: 2; x = x_hi * 2 + x_lo), y: 4, z: 16, core: 2. Of those that a mesh axis runs over, the one named last changes fastest.
Arguments:
- alm: bfloat16 [256, 256, 2, 1024], P('freq', ('grp', 'sub')), may hold values from -6 to 6
- band_index: int32 [32, 32], replicated, may hold values from 0 to 255
- band_weight: float32 [32, 32], replicated, may hold values from 0.05 to 0.5
- legendre: bfloat16 [256, 1024, 1024], P(('grp', 'sub')), may hold values from -0.0078125 to 0.0078125
- orders: int32 [256], replicated, may hold values from 0 to 1023, as said below
- owner: int32 [524288, 1], P(('grp', 'sub')), may hold values from 0 to 255; in each aligned block of 2048 rows (0 to 2047, 2048 to 4095, ...) at most 12 rows name the same one
- tile_local: int32 [524288], P(('grp', 'sub')), may hold values from 0 to 7
- interp: bfloat16 [524288, 512], P(('grp', 'sub')), may hold values from -0.25 to 0.25
Outputs:
- tod: bfloat16 [524288, 32], P(('grp', 'sub'), 'freq')
Inputs may be any that keep to these rules, and one draw needn't show every extreme that they name: 256 distinct orders; 0 and 1023 are always among them. `owner`: among the 2048 samples of one index of grp and sub (aligned blocks of 2048 rows) no cycle band is named more than 12 times, a bound that some block reaches.
All inputs are finite; a program needn't handle non-finite values.
Results may differ from a plain program's by a relative error of at most 0.0073.
Values may be sent and summed in bfloat16 or wider, within the bound.
A program may use at most 64 MiB of HBM per device.

v0:
```python
import math

import jax
import jax.numpy as jnp
from jax import lax
from jax.sharding import PartitionSpec as P

NPHI = 1024
TR = 4
TPHI = 128


def band_matrix(band_index, band_weight, first_freq, freq_count):
    freq_ids = first_freq + lax.iota(jnp.int32, freq_count)
    matches = (band_index[:, :, None] == freq_ids[None, None, :]).astype(jnp.float32)
    return jnp.sum(matches * band_weight[:, :, None], axis=1).astype(jnp.bfloat16)


def phase_basis(order_list, longitudes):
    lon_index = lax.iota(jnp.int32, longitudes)
    phase_turns = order_list[:, None] * lon_index[None, :] % longitudes
    angles = phase_turns.astype(jnp.float32) * (2.0 * math.pi / longitudes)
    factor = jnp.where(order_list == 0, 1.0, 2.0).astype(jnp.float32)[:, None]
    return jnp.stack([factor * jnp.cos(angles), -factor * jnp.sin(angles)]).astype(jnp.bfloat16)


def sample_values(weights, tile_ids, tiles):
    row_count = weights.shape[0]
    tile_total = tiles.shape[0]
    det_width = tiles.shape[1]
    pixel_count = tiles.shape[2]
    block_rows = min(256, row_count)
    flat_tiles = tiles.reshape(tile_total * det_width, pixel_count)

    def one_block(member):
        block_weights, block_ids = member
        products = lax.dot_general(
            block_weights, flat_tiles, (((1,), (1,)), ((), ())), preferred_element_type=jnp.float32
        )
        products = products.reshape(block_rows, tile_total, det_width)
        selector = (block_ids[:, None] == lax.iota(jnp.int32, tile_total)[None, :]).astype(
            jnp.float32
        )
        return jnp.sum(products * selector[:, :, None], axis=1)

    blocks = (
        weights.reshape(row_count // block_rows, block_rows, pixel_count),
        tile_ids.reshape(row_count // block_rows, block_rows),
    )
    return lax.map(one_block, blocks).reshape(row_count, det_width)


def on_device(alm, band_index, band_weight, legendre, orders, owner, tile_local, interp):
    freq_devices = lax.axis_size("freq")
    group_count = lax.axis_size("grp")
    sub_count = lax.axis_size("sub")
    owners_total = group_count * sub_count
    local_freqs = alm.shape[0]
    multipoles = alm.shape[3]
    cycle_total = legendre.shape[2]
    det_half = band_weight.shape[0] // freq_devices
    band_local = band_matrix(
        band_index, band_weight, lax.axis_index("freq") * local_freqs, local_freqs
    )
    flat_alm = alm.reshape(local_freqs, 2 * multipoles)
    partial_sums = jnp.dot(band_local, flat_alm, preferred_element_type=jnp.float32)
    detector_alm = lax.psum_scatter(partial_sums, "freq", scatter_dimension=0, tiled=True).astype(
        jnp.bfloat16
    )
    my_slot = lax.axis_index("grp") * sub_count + lax.axis_index("sub")
    my_order = orders[my_slot]
    degree = lax.iota(jnp.int32, multipoles)
    panel = jnp.where(degree[:, None] >= my_order, legendre[0], jnp.zeros_like(legendre[0]))
    cycle_coef = jnp.dot(
        detector_alm.reshape(det_half * 2, multipoles), panel, preferred_element_type=jnp.float32
    )
    cycle_coef = cycle_coef.astype(jnp.bfloat16).reshape(det_half, 1, 2, cycle_total)
    band_cycles = cycle_total // owners_total
    gathered = lax.all_to_all(
        lax.all_to_all(cycle_coef, "grp", split_axis=3, concat_axis=1, tiled=True),
        "sub",
        split_axis=3,
        concat_axis=1,
        tiled=True,
    )
    order_list = orders.reshape(group_count, sub_count).T.reshape(-1)
    basis = phase_basis(order_list, NPHI)
    sky = jnp.einsum("dmcr,cmj->drj", gathered, basis, preferred_element_type=jnp.float32).astype(
        jnp.bfloat16
    )
    cycle_tiles = band_cycles // TR
    lon_tiles = NPHI // TPHI
    tiles = sky.reshape(det_half, cycle_tiles, TR, lon_tiles, TPHI).transpose(1, 3, 0, 2, 4)
    tiles = tiles.reshape(cycle_tiles * lon_tiles, det_half, TR * TPHI)
    sample_count = interp.shape[0]
    pixel_count = interp.shape[1]
    capacity = max(2, 3 * sample_count // (2 * owners_total))
    target = owner[:, 0]
    owner_marks = (target[:, None] == lax.iota(jnp.int32, owners_total)[None, :]).astype(jnp.int32)
    running = jnp.cumsum(owner_marks, axis=0)
    slot_rank = jnp.sum(running * owner_marks, axis=1) - 1
    slot_index = target * capacity + slot_rank
    send_weights = (
        jnp.zeros((owners_total * capacity, pixel_count), jnp.bfloat16).at[slot_index].set(interp)
    )
    send_ids = jnp.full((owners_total * capacity,), -1, jnp.int32).at[slot_index].set(tile_local)
    send_weights = send_weights.reshape(group_count, sub_count, capacity, pixel_count)
    send_ids = send_ids.reshape(group_count, sub_count, capacity)
    got_weights, got_ids = (
        lax.all_to_all(
            lax.all_to_all(send_weights, "grp", split_axis=0, concat_axis=0, tiled=True),
            "sub",
            split_axis=1,
            concat_axis=1,
            tiled=True,
        ),
        lax.all_to_all(
            lax.all_to_all(send_ids, "grp", split_axis=0, concat_axis=0, tiled=True),
            "sub",
            split_axis=1,
            concat_axis=1,
            tiled=True,
        ),
    )
    values = sample_values(got_weights.reshape(-1, pixel_count), got_ids.reshape(-1), tiles)
    values = values.astype(jnp.bfloat16).reshape(group_count, sub_count, capacity, det_half)
    returned = lax.all_to_all(
        lax.all_to_all(values, "grp", split_axis=0, concat_axis=0, tiled=True),
        "sub",
        split_axis=1,
        concat_axis=1,
        tiled=True,
    )
    table = returned.reshape(owners_total * capacity, det_half)
    return table[slot_index]


def solution(mesh):
    placed = (
        P("freq", ("grp", "sub"), None, None),
        P(),
        P(),
        P(("grp", "sub"), None, None),
        P(),
        P(("grp", "sub"), None),
        P(("grp", "sub")),
        P(("grp", "sub"), None),
    )
    return jax.shard_map(
        on_device, mesh=mesh, in_specs=placed, out_specs=P(("grp", "sub"), "freq"), check_vma=False
    )
```

profile of v0, /device:TPU:1, one launch (start us, length us, event | category | flops | bytes accessed | tf_op | source)
XLA Modules:
  0.0 358.8 jit_solution(15337952053953467474)
XLA Ops:
  12.7 8.2 %scatter_custom_fusion.1 = s32[3072]{0:T(1024)S(1)} fusion(s32[2048]{0:T(1024)S(1)} %bitcast.114, s32[2048]{0:T(1024)} %param.16, s32[]{:T(128)} %constant.34.clone.1), kind=kCustom, calls=%fused_computation.50 | custom fusion | bytes 12800 | tf_op jit(solution)/shard_map/scatter | solution.py:106
  21.8 15.7 %all-to-all-start.4 = ((s32[16,1,192]{2,1,0:T(1,128)}), s32[16,1,192]{2,1,0:T(1,128)S(1)}, u32[]{:S(2)}, u32[]{:S(2)}) async-start(s32[16,1,192]{2,1,0:T(1,128)} %reshape.320), calls=%async_computation.5 | async-start | bytes 32768 | tf_op jit(solution)/shard_map/all_to_all | solution.py:118
  38.8 10.1 %all-to-all-done.4 = s32[16,1,192]{2,1,0:T(1,128)S(1)} async-done(((s32[16,1,192]{2,1,0:T(1,128)}), s32[16,1,192]{2,1,0:T(1,128)S(1)}, u32[]{:S(2)}, u32[]{:S(2)}) %all-to-all-start.4) | async-done | bytes 12320 | tf_op jit(solution)/shard_map/all_to_all | solution.py:118
  51.0 7.5 %all-to-all-start.5 = ((s32[16,1,192]{2,1,0:T(1,128)}), s32[16,1,192]{2,1,0:T(1,128)S(1)}, u32[]{:S(2)}, u32[]{:S(2)}) async-start(s32[16,1,192]{2,1,0:T(1,128)} %reshape.322), calls=%async_computation.6 | async-start | bytes 32768 | tf_op jit(solution)/shard_map/all_to_all | solution.py:117
  59.4 2.1 fusion.15
  64.2 3.5 all-to-all-start.2
  67.7 11.2 %scatter_custom_fusion = bf16[3072,512]{1,0:T(8,128)(2,1)S(1)} fusion(s32[2048]{0:T(1024)S(1)} %bitcast.115, bf16[2048,512]{1,0:T(8,128)(2,1)} %param.17, bf16[]{:T(256)} %constant.31.clone.1), kind=kCustom, calls=%fused_computation.25 | custom fusion | bytes 3146240 | tf_op jit(solution)/shard_map/scatter | solution.py:104
  78.9 2.7 reshape.275
  81.6 6.0 %copy.51 = bf16[16,16,12,512]{3,1,2,0:T(8,128)(2,1)} copy(bf16[16,16,12,512]{3,2,1,0:T(8,128)(2,1)} %reshape.275) | data formatting | bytes 6291456 | tf_op jit(solution)/shard_map/reshape | solution.py:107
  87.6 11.4 %all-to-all-start = ((bf16[16,16,12,512]{3,1,2,0:T(8,128)(2,1)}), bf16[16,16,12,512]{3,1,2,0:T(8,128)(2,1)S(1)}, u32[]{:S(2)}, u32[]{:S(2)}) async-start(bf16[16,16,12,512]{3,1,2,0:T(8,128)(2,1)} %copy.51), calls=%async_computation | async-start | bytes 6291456 | tf_op jit(solution)/shard_map/all_to_all | solution.py:111
  100.1 2.3 copy.71
  102.4 1.9 bitcast_bitcast_fusion
  104.3 2.2 reshape.318
  106.5 129.3 %all-to-all-done = bf16[16,16,12,512]{3,1,2,0:T(8,128)(2,1)S(1)} async-done(((bf16[16,16,12,512]{3,1,2,0:T(8,128)(2,1)}), bf16[16,16,12,512]{3,1,2,0:T(8,128)(2,1)S(1)}, u32[]{:S(2)}, u32[]{:S(2)}) %all-to-all-start) | async-done | bytes 3145760 | tf_op jit(solution)/shard_map/all_to_all | solution.py:111
  235.8 7.8 %all-to-all-start.3 = ((bf16[16,2,1024]{2,1,0:T(2,128)(2,1)}), bf16[16,2,1024]{2,1,0:T(2,128)(2,1)S(1)}, u32[]{:S(2)}, u32[]{:S(2)}) async-start(bf16[16,2,1024]{2,1,0:T(2,128)(2,1)} %reshape.318), calls=%async_computation.4 | async-start | bytes 131072 | tf_op jit(solution)/shard_map/all_to_all | solution.py:79
  243.6 3.4 copy.52
  247.0 2.4 all-to-all-done.3
  249.5 4.0 %all-to-all-start.1 = ((bf16[16,16,12,512]{3,0,2,1:T(8,128)(2,1)}), bf16[16,16,12,512]{3,0,2,1:T(8,128)(2,1)S(1)}, u32[]{:S(2)}, u32[]{:S(2)}) async-start(bf16[16,16,12,512]{3,0,2,1:T(8,128)(2,1)} %copy.52), calls=%async_computation.1 | async-start | bytes 6291456 | tf_op jit(solution)/shard_map/all_to_all | solution.py:110
  253.7 5.7 %multiply_convert_fusion.1 = (bf16[1,256,1024]{2,1,0:T(8,128)(2,1)}, bf16[1,256,1024]{2,1,0:T(8,128)(2,1)}) fusion(s32[256]{0:T(256)S(1)} %reshape.280, f32[256]{0:T(256)S(1)} %get-tuple-element.45, f32[256]{0:T(256)S(1)} %get-tuple-element.46), kind=kLoop, calls=%fused_computation.37 | loop fusion | flops 4718592 | bytes 1051648 | tf_op jit(solution)/shard_map/convert
  261.4 2.2 copy.58
  263.6 1.5 all_to_all.53
  265.1 1.5 fusion.14
  266.8 25.1 %all-to-all-done.1 = bf16[16,16,12,512]{3,0,2,1:T(8,128)(2,1)S(1)} async-done(((bf16[16,16,12,512]{3,0,2,1:T(8,128)(2,1)}), bf16[16,16,12,512]{3,0,2,1:T(8,128)(2,1)S(1)}, u32[]{:S(2)}, u32[]{:S(2)}) %all-to-all-start.1) | async-done | bytes 3145760 | tf_op jit(solution)/shard_map/all_to_all | solution.py:110
  291.9 3.8 %copy.53 = bf16[16,16,12,512]{3,2,1,0:T(8,128)(2,1)} copy(bf16[16,16,12,512]{3,0,2,1:T(8,128)(2,1)S(1)} %all-to-all-done.1) | data formatting | bytes 6291456 | tf_op jit(solution)/shard_map/all_to_all | solution.py:110
  295.7 4.8 %reshape_reshape.9 = bf16[12,256,512]{2,1,0:T(8,128)(2,1)S(1)} reshape(bf16[16,16,12,512]{3,2,1,0:T(8,128)(2,1)} %copy.53) | data formatting | bytes 6291456 | tf_op jit(solution)/shard_map/reshape;reshape | solution.py:47
  300.5 3.6 while.10
  304.1 2.5 convert_element_type.54
  306.5 2.1 copy.64
  309.5 19.8 %all_to_all.66 = bf16[16,2,1536]{2,1,0:T(2,128)(2,1)S(1)} all-to-all(bf16[16,2,1536]{2,1,0:T(2,128)(2,1)S(1)} %reshape.324), channel_id=1, replica_groups=mesh['freq'=2,'grp'=16,'sub'=16] {'grp'}, dimensions={0} | all-to-all | bytes 196608 | tf_op jit(solution)/shard_map/all_to_all | solution.py:128
  331.8 6.1 %all-to-all-start.7 = ((bf16[16,2,1536]{2,1,0:T(2,128)(2,1)}), bf16[16,2,1536]{2,1,0:T(2,128)(2,1)S(1)}, u32[]{:S(2)}, u32[]{:S(2)}) async-start(bf16[16,2,1536]{2,1,0:T(2,128)(2,1)} %reshape.326), calls=%async_computation.8 | async-start | bytes 196608 | tf_op jit(solution)/shard_map/all_to_all | solution.py:127
  337.9 5.9 %all-to-all-done.7 = bf16[16,2,1536]{2,1,0:T(2,128)(2,1)S(1)} async-done(((bf16[16,2,1536]{2,1,0:T(2,128)(2,1)}), bf16[16,2,1536]{2,1,0:T(2,128)(2,1)S(1)}, u32[]{:S(2)}, u32[]{:S(2)}) %all-to-all-start.7) | async-done | bytes 98336 | tf_op jit(solution)/shard_map/all_to_all | solution.py:127
  345.0 6.2 %gather_fusion = bf16[2048,16]{1,0:T(8,128)(2,1)S(1)} fusion(bf16[3072,16]{1,0:T(8,128)(2,1)S(1)} %reshape.311, s32[2048]{0:T(1024)S(1)} %broadcast_clamp_fusion), kind=kCustom, calls=%fused_computation | custom fusion | bytes 139264 | tf_op jit(solution)/shard_map/gather | solution.py:135
  (111 shorter events, 25.8 us)
Async XLA Ops:
  6.5 3.2 copy-start.1
  6.5 51.9 %reduce-scatter.2.cloned.1.call-start = ((), (), s32[]{:S(2)}) async-start(), calls=%async_computation.9 | async-start | bytes 393216 | tf_op jit(solution)/shard_map/reduce_scatter | solution.py:67
  11.7 25.8 %copy-start.2 = (s32[256]{0:T(256)S(1)}, s32[256]{0:T(256)}, u32[]{:S(2)}) copy-start(s32[256]{0:T(256)} %param.14) | copy-start | bytes 3076
  21.8 27.1 %all-to-all-start.4 = ((s32[16,1,192]{2,1,0:T(1,128)}), s32[16,1,192]{2,1,0:T(1,128)S(1)}, u32[]{:S(2)}, u32[]{:S(2)}) async-start(s32[16,1,192]{2,1,0:T(1,128)} %reshape.320), calls=%async_computation.5 | async-start | bytes 32768 | tf_op jit(solution)/shard_map/all_to_all | solution.py:118
  51.0 13.3 %all-to-all-start.5 = ((s32[16,1,192]{2,1,0:T(1,128)}), s32[16,1,192]{2,1,0:T(1,128)S(1)}, u32[]{:S(2)}, u32[]{:S(2)}) async-start(s32[16,1,192]{2,1,0:T(1,128)} %reshape.322), calls=%async_computation.6 | async-start | bytes 32768 | tf_op jit(solution)/shard_map/all_to_all | solution.py:117
  64.2 23.4 %all-to-all-start.2 = ((bf16[16,2,1024]{2,1,0:T(2,128)(2,1)}), bf16[16,2,1024]{2,1,0:T(2,128)(2,1)S(1)}, u32[]{:S(2)}, u32[]{:S(2)}) async-start(bf16[16,2,1024]{2,1,0:T(2,128)(2,1)} %reshape.316), calls=%async_computation.3 | async-start | bytes 131072 | tf_op jit(solution)/shard_map/all_to_all | solution.py:80
  87.6 148.2 %all-to-all-start = ((bf16[16,16,12,512]{3,1,2,0:T(8,128)(2,1)}), bf16[16,16,12,512]{3,1,2,0:T(8,128)(2,1)S(1)}, u32[]{:S(2)}, u32[]{:S(2)}) async-start(bf16[16,16,12,512]{3,1,2,0:T(8,128)(2,1)} %copy.51), calls=%async_computation | async-start | bytes 6291456 | tf_op jit(solution)/shard_map/all_to_all | solution.py:111
  235.8 13.7 %all-to-all-start.3 = ((bf16[16,2,1024]{2,1,0:T(2,128)(2,1)}), bf16[16,2,1024]{2,1,0:T(2,128)(2,1)S(1)}, u32[]{:S(2)}, u32[]{:S(2)}) async-start(bf16[16,2,1024]{2,1,0:T(2,128)(2,1)} %reshape.318), calls=%async_computation.4 | async-start | bytes 131072 | tf_op jit(solution)/shard_map/all_to_all | solution.py:79
  249.5 42.4 %all-to-all-start.1 = ((bf16[16,16,12,512]{3,0,2,1:T(8,128)(2,1)}), bf16[16,16,12,512]{3,0,2,1:T(8,128)(2,1)S(1)}, u32[]{:S(2)}, u32[]{:S(2)}) async-start(bf16[16,16,12,512]{3,0,2,1:T(8,128)(2,1)} %copy.52), calls=%async_computation.1 | async-start | bytes 6291456 | tf_op jit(solution)/shard_map/all_to_all | solution.py:110
  295.6 4.8 %copy-start = (bf16[12,256,16]{1,2,0:T(8,128)(2,1)S(1)}, bf16[12,256,16]{1,2,0:T(8,128)(2,1)}, u32[]{:S(2)}) copy-start(bf16[12,256,16]{1,2,0:T(8,128)(2,1)} %custom-call.2) | copy-start | bytes 294916
  331.8 12.0 %all-to-all-start.7 = ((bf16[16,2,1536]{2,1,0:T(2,128)(2,1)}), bf16[16,2,1536]{2,1,0:T(2,128)(2,1)S(1)}, u32[]{:S(2)}, u32[]{:S(2)}) async-start(bf16[16,2,1536]{2,1,0:T(2,128)(2,1)} %reshape.326), calls=%async_computation.8 | async-start | bytes 196608 | tf_op jit(solution)/shard_map/all_to_all | solution.py:127
Sparse Core Ops, SparseCore 0:
  10.1 28.6 reduce-scatter.1
where the time goes:
time: 360 us; the launch traced here: 359 us
  waiting for transfers between devices  174 us (48%)
  local copies, waits for them, and re-layouts  76.5 us (21%)
  starting transfers between devices  56 us (16%)
  blocking collectives  19.8 us (6%)
  between operations  13.8 us (4%)
  other arithmetic  11.1 us (3%)
  matrix products  7.29 us (2%)
    all_to_all x1, waiting for transfers between devices, on_device(): lax.all_to_all(send_weights, 'grp', split_axis=0, concat_axis=0, tiled=True)  129 us
    all_to_all x1, waiting for transfers between devices, on_device(): lax.all_to_all(lax.all_to_all(send_weights, 'grp', split_axis=0, concat_a...  25.1 us
    all_to_all x1, blocking collectives, on_device(): lax.all_to_all(values, 'grp', split_axis=0, concat_axis=0, tiled=True)  19.8 us
    all_to_all x1, starting transfers between devices, on_device(): lax.all_to_all(send_ids, 'grp', split_axis=0, concat_axis=0, tiled=True)  15.7 us
    unnamed x22, local copies, waits for them, and re-layouts  13.9 us
    all_to_all x1, starting transfers between devices, on_device(): lax.all_to_all(send_weights, 'grp', split_axis=0, concat_axis=0, tiled=True)  11.4 us
    scatter x1, local copies, waits for them, and re-layouts, on_device(): jnp.zeros((owners_total * capacity, pixel_count), jnp.bfloat16)  11.2 us
    all_to_all x1, waiting for transfers between devices, on_device(): lax.all_to_all(send_ids, 'grp', split_axis=0, concat_axis=0, tiled=True)  10.1 us
  transfers between devices with their start and end apart: 8, of which 6 were waited for; matrix products, arithmetic and copies ran while one was open for 17% of the time, Pallas kernels for 0%

commit v1 on v0

v1 whole, which is shorter than its diff:
```python
import math

import jax
import jax.numpy as jnp
import numpy as np
from jax import lax
from jax.experimental import pallas as pl
from jax.experimental.pallas import tpu as pltpu
from jax.sharding import PartitionSpec as P

MESH = pl.DeviceIdType.MESH
F32, BF16, I32 = jnp.float32, jnp.bfloat16, jnp.int32
NF, NG, NS = 2, 16, 16
DET = 32
HALF_DET = DET // NF
L = 1024
RH = 512
NPHI = 1024
SD = 2048
PIX = 512
CAP = 12
NJ = 8
ROWS = NJ * CAP
GROUP = ROWS // 2
HALF_LANES = NS * GROUP
LANES = 2 * HALF_LANES
NN = (((1,), (0,)), ((), ()))
NT = (((1,), (1,)), ((), ()))
TN = (((0,), (0,)), ((), ()))


def dot(a, b, dims=NN):
    return lax.dot_general(a, b, dims, preferred_element_type=F32)


def lane_table():
    lane = np.arange(LANES)
    g, rest = lane // HALF_LANES, lane % HALF_LANES
    s, j4, k = rest // GROUP, rest % GROUP // CAP, rest % CAP
    table = np.zeros((8, LANES), np.int32)
    table[0] = s * NJ + g * 4 + j4
    table[1] = k
    table[2] = g * 4 + j4
    table[3] = s * 16 + k
    table[4] = j4 * 8
    return table


def kernel(
    order_ref, part_ref, leg_ref, int_ref, own_ref, tile_ref, ordb_ref, tab_ref, out_ref,
    part_s, part_r, leg_v, int_v, pick, d_s, d_r, y_s, y_r, y_f, coef, basis, acc, tiles,
    v_s, v_r, cols, sel_v, sel_s, rank_v,
    loc_sem, ex_sem, ys_sem, yr_sem, ds_sem, dr_sem, rs_sem, rr_sem, vs_sem, vr_sem,
):
    f, z, s = lax.axis_index("freq"), lax.axis_index("grp"), lax.axis_index("sub")
    me = f * NS + s

    leg_copy = pltpu.make_async_copy(
        leg_ref.at[0, :, pl.ds(pl.multiple_of(f * RH, RH), RH)], leg_v, loc_sem.at[0]
    )
    int_copy = pltpu.make_async_copy(int_ref, int_v, loc_sem.at[1])
    leg_copy.start()
    int_copy.start()

    barrier = pltpu.get_barrier_semaphore()

    def greet(k, _):
        other = lax.rem(me + k, NF * NS)
        pl.semaphore_signal(
            barrier, inc=1, device_id=(other // NS, z, lax.rem(other, NS)), device_id_type=MESH
        )
        return 0

    lax.fori_loop(1, NF * NS, greet, 0)
    up, down = lax.rem(z + 1, NG), lax.rem(z + NG - 1, NG)
    for zz in (up, down):
        pl.semaphore_signal(barrier, inc=1, device_id=(f, zz, s), device_id_type=MESH)
    part_s[...] = part_ref[...].astype(BF16)
    pl.semaphore_wait(barrier, NF * NS - 1 + 2)

    exchange = pltpu.make_async_remote_copy(
        src_ref=part_s, dst_ref=part_r, send_sem=ex_sem.at[0], recv_sem=ex_sem.at[1],
        device_id=(1 - f, z, s), device_id_type=MESH,
    )
    exchange.start()

    lane = lax.broadcasted_iota(I32, (128, 128), 1)
    row = lax.broadcasted_iota(I32, (128, 128), 0)
    before = (row < lane).astype(BF16)
    band_row = lax.broadcasted_iota(I32, (NF * NS * NJ, 128), 0)
    rank_row = lax.broadcasted_iota(I32, (16, 128), 0)
    seen = jnp.zeros((NF * NS * NJ, 1), F32)
    slot_tile = jnp.zeros((16, NF * NS * NJ), F32)
    for c in range(SD // 128):
        named = band_row == own_ref[c : c + 1, :]
        ones = jnp.where(named, 1.0, 0.0)
        marks = ones.astype(BF16)
        count = dot(marks, before) + seen
        rank = jnp.sum(jnp.where(named, count, 0.0), axis=0, keepdims=True)
        seen = seen + jnp.sum(ones, axis=1, keepdims=True)
        rank_i = rank.astype(I32)
        rank_v[c : c + 1, :] = rank_i
        ids = jnp.where(rank_row == rank_i, tile_ref[c : c + 1, :].astype(F32), 0.0)
        slot_tile = slot_tile + dot(ids.astype(BF16), marks, NT)
    half_tile = jnp.where(f == 0, slot_tile[:, :128], slot_tile[:, 128:])
    lane16 = lax.broadcasted_iota(I32, (16, 128), 1)
    mine16 = lane16 // NJ == s

    def put_tiles(other, _):
        turned = pltpu.roll(half_tile, lax.rem(s - other + NS, NS) * NJ, 1)
        y_s[other, 16:32, :] = jnp.where(mine16, turned, 0.0).astype(BF16)
        return 0

    lax.fori_loop(0, NS, put_tiles, 0)

    int_copy.wait()
    slot_row = lax.broadcasted_iota(I32, (4 * ROWS, 128), 0)

    def pack(q, _):
        wanted = slot_row + q * (4 * ROWS)
        for c in range(SD // 128):
            key = (own_ref[c : c + 1, :] - f * 128) * CAP + rank_v[c : c + 1, :]
            pick[:, c * 128 : (c + 1) * 128] = jnp.where(wanted == key, 1.0, 0.0).astype(BF16)
        packed = dot(pick[...], int_v[...]).astype(BF16)
        for n in range(4):
            d_s[q * 4 + n] = packed[n * ROWS : (n + 1) * ROWS, :]
        return 0

    lax.fori_loop(0, 4, pack, 0)

    exchange.wait_recv()
    total = part_ref[...] + part_r[...].astype(F32)
    degree = lax.rem(lax.broadcasted_iota(I32, (DET, 2 * L), 1), L)
    total = jnp.where(degree >= order_ref[z * NS + s], total, 0.0).astype(BF16)
    leg_copy.wait()
    cyc = dot(jnp.concatenate([total[:, :L], total[:, L:]], axis=0), leg_v[...])
    turn = lax.broadcasted_iota(I32, (DET, RH), 1) & 3
    quads = (
        lax.broadcasted_iota(I32, (128, RH), 1) // 4 == lax.broadcasted_iota(I32, (128, RH), 0)
    ).astype(BF16)
    halves = []
    for c in range(2):
        one = cyc[c * DET : (c + 1) * DET, :]
        spread = jnp.concatenate([jnp.where(turn == i, one, 0.0) for i in range(4)], axis=0)
        halves.append(dot(quads, spread.astype(BF16), NT).reshape(NS, NJ, 128))
    y_s[:, 0:16, :] = jnp.concatenate(halves, axis=1).astype(BF16)

    def y_copy(k, dst):
        return pltpu.make_async_remote_copy(
            src_ref=y_s.at[lax.rem(s + k, NS)], dst_ref=y_r.at[dst],
            send_sem=ys_sem.at[k], recv_sem=yr_sem.at[k],
            device_id=(f, z, lax.rem(s + k, NS)), device_id_type=MESH,
        )

    def d_copy(k, dst):
        return pltpu.make_async_remote_copy(
            src_ref=d_s.at[lax.rem(s + k, NS)], dst_ref=d_r.at[dst],
            send_sem=ds_sem.at[k], recv_sem=dr_sem.at[k],
            device_id=(f, z, lax.rem(s + k, NS)), device_id_type=MESH,
        )

    def start_y(k, _):
        y_copy(k, s).start()
        return 0

    def start_d(k, _):
        d_copy(k, s).start()
        return 0

    lax.fori_loop(1, NS, start_y, 0)
    lax.fori_loop(1, NS, start_d, 0)
    y_r[s] = y_s[s]
    d_r[s] = d_s[s]

    def make_basis(p, _):
        hops = (p + 1) // 2
        zz = lax.rem(z + NG + (1 - 2 * lax.rem(p, 2)) * hops, NG)
        orders = ordb_ref[pl.ds(pl.multiple_of(zz * NS, NS), NS), :]
        lon = lax.broadcasted_iota(I32, (NS, 128), 1)
        fine = ((orders * lon) & (NPHI - 1)).astype(F32) * (2.0 * math.pi / NPHI)
        coarse = ((orders * (lon * 128)) & (NPHI - 1)).astype(F32) * (2.0 * math.pi / NPHI)
        weight = jnp.where(orders == 0, 1.0, 2.0)
        cos_u, sin_u = weight * jnp.cos(fine), weight * jnp.sin(fine)
        cos_t, sin_t = jnp.cos(coarse), jnp.sin(coarse)
        top = pl.multiple_of(p * 32, 32)
        for t in range(8):
            ct, st = cos_t[:, t : t + 1], sin_t[:, t : t + 1]
            basis[pl.ds(top, NS), t * 128 : (t + 1) * 128] = (ct * cos_u - st * sin_u).astype(BF16)
            basis[pl.ds(top + NS, NS), t * 128 : (t + 1) * 128] = (-(st * cos_u + ct * sin_u)).astype(BF16)
        return 0

    lax.fori_loop(0, NG, make_basis, 0)

    sel_s[...] = (lax.broadcasted_iota(I32, (256, LANES), 0) == tab_ref[3:4, :]).astype(BF16)
    cols[...] = jnp.zeros_like(cols)
    cols[0:16, :] = ((own_ref[...] // NJ) * 16 + rank_v[...]).astype(F32)
    cols[16:32, :] = (own_ref[...] & (NJ - 1)).astype(F32)
    turned_cols = cols[...].T
    place = lax.broadcasted_iota(I32, (128, NF * NS * 16), 1).astype(F32)
    for c in range(SD // 128):
        sel_v[c * 128 : (c + 1) * 128, :] = (place == turned_cols[:, c : c + 1]).astype(BF16)

    def wait_y(k, _):
        y_copy(k, lax.rem(s + NS - k, NS)).wait_recv()
        return 0

    lax.fori_loop(1, NS, wait_y, 0)
    y_f[...] = y_r[:, 0:16, :].astype(F32).reshape(NS * 16, 128)
    for c in range(2):
        for j in range(NJ):
            coef[c * 16 : (c + 1) * 16, j * 128 : (j + 1) * 128] = y_f[
                pl.ds(c * NJ + j, NS, stride=16), :
            ].astype(BF16)

    def ring(k, way):
        source = 0 if k == 1 else 2 * (k - 1) - (way == 0)
        target = 2 * k - (way == 0)
        return pltpu.make_async_remote_copy(
            src_ref=coef.at[pl.ds(source * 32, 32), :], dst_ref=coef.at[pl.ds(target * 32, 32), :],
            send_sem=rs_sem.at[target], recv_sem=rr_sem.at[target],
            device_id=(f, up if way == 0 else down, s), device_id_type=MESH,
        )

    def sky_first(j, _):
        at = pl.multiple_of(j * 128, 128)
        acc[pl.ds(at, 128), :] = dot(coef[0:256, pl.ds(at, 128)], basis[0:256, :], TN)
        return 0

    for k in range(1, 9):
        ways = (0, 1) if k < 8 else (0,)
        for way in ways:
            ring(k, way).start()
        if k >= 5:
            lax.fori_loop((k - 5) * 2, (k - 4) * 2, sky_first, 0)
        for way in ways:
            ring(k, way).wait_recv()

    def sky_last(j, _):
        at = pl.multiple_of(j * 128, 128)
        sky = acc[pl.ds(at, 128), :] + dot(coef[256:512, pl.ds(at, 128)], basis[256:512, :], TN)
        sky = sky.astype(BF16)
        for i in range(4):
            for t in range(8):
                tiles[j, t * DET : (t + 1) * DET, i * 128 : (i + 1) * 128] = sky[
                    i * DET : (i + 1) * DET, t * 128 : (t + 1) * 128
                ]
        return 0

    lax.fori_loop(0, NJ, sky_last, 0)

    tile_sum = jnp.sum(y_r[:, 16:32, :].astype(F32), axis=0).astype(BF16)
    here = (lax.broadcasted_iota(I32, (128, LANES), 0) == tab_ref[0:1, :]).astype(BF16)
    by_rank = dot(tile_sum, here)
    own_rank = lax.broadcasted_iota(I32, (16, LANES), 0) == tab_ref[1:2, :]
    code = jnp.sum(jnp.where(own_rank, by_rank, 0.0), axis=0, keepdims=True).astype(I32)
    code = code + tab_ref[4:5, :]

    def wait_d(k, _):
        d_copy(k, lax.rem(s + NS - k, NS)).wait_recv()
        return 0

    lax.fori_loop(1, NS, wait_d, 0)
    sums = []
    for g in range(2):
        weights = d_r[:, g * GROUP : (g + 1) * GROUP, :].reshape(HALF_LANES, PIX)
        picked = code[:, g * HALF_LANES : (g + 1) * HALF_LANES]

        def one_band(j, value, g=g, weights=weights, picked=picked):
            every = dot(tiles[g * 4 + j], weights, NT)
            for t in range(8):
                value = value + jnp.where(
                    picked == j * 8 + t, every[t * DET : (t + 1) * DET, :], 0.0
                )
            return value

        sums.append(lax.fori_loop(0, 4, one_band, jnp.zeros((DET, HALF_LANES), F32)))
    value = jnp.concatenate(sums, axis=1)
    band = tab_ref[2:3, :]
    spread = jnp.concatenate(
        [
            jnp.where(band == j, value[h * HALF_DET : (h + 1) * HALF_DET, :], 0.0).astype(BF16)
            for h in range(NF)
            for j in range(NJ)
        ],
        axis=0,
    )
    together = dot(sel_s[...], spread, NT).astype(BF16)
    for h in range(NF):
        v_s[h] = together[:, h * 128 : (h + 1) * 128].reshape(NS, 16, 128)

    def v_copy(k, dst):
        other = lax.rem(me + k, NF * NS)
        oh, os = other // NS, lax.rem(other, NS)
        return pltpu.make_async_remote_copy(
            src_ref=v_s.at[oh, os], dst_ref=v_r.at[dst],
            send_sem=vs_sem.at[k], recv_sem=vr_sem.at[k],
            device_id=(oh, z, os), device_id_type=MESH,
        )

    def start_v(k, _):
        v_copy(k, me).start()
        return 0

    def wait_v(k, _):
        v_copy(k, lax.rem(me + NF * NS - k, NF * NS)).wait_recv()
        return 0

    lax.fori_loop(1, NF * NS, start_v, 0)
    v_r[me] = v_s[f, s]
    lax.fori_loop(1, NF * NS, wait_v, 0)

    found = dot(sel_v[...], v_r[...].reshape(NF * NS * 16, 128))
    fold = ((row & (HALF_DET - 1)) == lane).astype(BF16)
    lane_band = (lane // HALF_DET).astype(F32)
    for c in range(SD // 128):
        kept = jnp.where(
            lane_band == turned_cols[:, 16 + c : 17 + c], found[c * 128 : (c + 1) * 128, :], 0.0
        )
        out_ref[c * 128 : (c + 1) * 128, :] = dot(kept.astype(BF16), fold)[:, :HALF_DET].astype(BF16)

    exchange.wait_send()

    def sent(k, _):
        y_copy(k, s).wait_send()
        d_copy(k, s).wait_send()
        return 0

    def sent_v(k, _):
        v_copy(k, me).wait_send()
        return 0

    lax.fori_loop(1, NS, sent, 0)
    lax.fori_loop(1, NF * NS, sent_v, 0)
    for k in range(1, 9):
        for way in (0, 1) if k < 8 else (0,):
            ring(k, way).wait_send()


def band_matrix(band_index, band_weight, first_freq, freq_count):
    freq_ids = first_freq + lax.iota(I32, freq_count)
    matches = (band_index[:, :, None] == freq_ids[None, None, :]).astype(F32)
    return jnp.sum(matches * band_weight[:, :, None], axis=1).astype(BF16)


def on_device(alm, band_index, band_weight, legendre, orders, owner, tile_local, interp):
    freqs = alm.shape[0]
    band = band_matrix(band_index, band_weight, lax.axis_index("freq") * freqs, freqs)
    part = jnp.dot(band, alm.reshape(freqs, 2 * L), preferred_element_type=F32)
    order_rows = jnp.broadcast_to(orders[:, None], (orders.shape[0], 128))
    dma = pltpu.SemaphoreType.DMA
    vmem = pl.BlockSpec(memory_space=pltpu.VMEM)
    anywhere = pl.BlockSpec(memory_space=pl.ANY)
    return pl.pallas_call(
        kernel,
        out_shape=jax.ShapeDtypeStruct((SD, HALF_DET), BF16),
        in_specs=[
            pl.BlockSpec(memory_space=pltpu.SMEM), vmem, anywhere, anywhere, vmem, vmem, vmem, vmem,
        ],
        out_specs=vmem,
        scratch_shapes=[
            pltpu.VMEM((DET, 2 * L), BF16),
            pltpu.VMEM((DET, 2 * L), BF16),
            pltpu.VMEM((L, RH), BF16),
            pltpu.VMEM((SD, PIX), BF16),
            pltpu.VMEM((4 * ROWS, SD), BF16),
            pltpu.VMEM((NS, ROWS, PIX), BF16),
            pltpu.VMEM((NS, ROWS, PIX), BF16),
            pltpu.VMEM((NS, 32, 128), BF16),
            pltpu.VMEM((NS, 32, 128), BF16),
            pltpu.VMEM((NS * 16, 128), F32),
            pltpu.VMEM((NG * 32, 1024), BF16),
            pltpu.VMEM((NG * 32, NPHI), BF16),
            pltpu.VMEM((1024, NPHI), F32),
            pltpu.VMEM((NJ, 8 * DET, PIX), BF16),
            pltpu.VMEM((NF, NS, 16, 128), BF16),
            pltpu.VMEM((NF * NS, 16, 128), BF16),
            pltpu.VMEM((128, 128), F32),
            pltpu.VMEM((SD, NF * NS * 16), BF16),
            pltpu.VMEM((256, LANES), BF16),
            pltpu.VMEM((16, 128), I32),
            dma((2,)), dma((2,)), dma((NS,)), dma((NS,)), dma((NS,)), dma((NS,)),
            dma((NG,)), dma((NG,)), dma((NF * NS,)), dma((NF * NS,)),
        ],
        compiler_params=pltpu.CompilerParams(
            collective_id=0, has_side_effects=True, vmem_limit_bytes=48 * 2**20
        ),
    )(
        orders, part, legendre, interp, owner.reshape(16, 128), tile_local.reshape(16, 128),
        order_rows, jnp.asarray(lane_table()),
    )


def solution(mesh):
    placed = (
        P("freq", ("grp", "sub"), None, None),
        P(),
        P(),
        P(("grp", "sub"), None, None),
        P(),
        P(("grp", "sub"), None),
        P(("grp", "sub")),
        P(("grp", "sub"), None),
    )
    return jax.shard_map(
        on_device, mesh=mesh, in_specs=placed, out_specs=P(("grp", "sub"), "freq"), check_vma=False
    )
```

time: 360 us -> 90.4 us (0.25)
  waiting for transfers between devices: 174 us -> 0 us
  Pallas kernels: 0 us -> 79.8 us
  local copies, waits for them, and re-layouts: 76.5 us -> 8.79 us
  starting transfers between devices: 56 us -> 0 us
  blocking collectives: 19.8 us -> 0 us
  between operations: 13.8 us -> 0.05 us
  other arithmetic: 11.1 us -> 1.09 us
  matrix products: 7.29 us -> 0.2 us
    all_to_all x7 -> x0, waiting for transfers between devices: 174 us -> none  [the longest x1 129 us: on_device(): lax.all_to_all(send_weights, 'grp', split_axis=0, concat_axis=0, tiled=True)]
    pallas_call x0 -> x1, Pallas kernels: none -> 79.8 us  [on_device(): pl.pallas_call(kernel, out_shape=jax.ShapeDtypeStruct((SD, HALF_DET), BF1...]
    all_to_all x7 -> x0, starting transfers between devices: 56 us -> none  [the longest x1 15.7 us: on_device(): lax.all_to_all(send_ids, 'grp', split_axis=0, concat_axis=0, tiled=True)]
    all_to_all x1 -> x0, blocking collectives: 19.8 us -> none  [on_device(): lax.all_to_all(values, 'grp', split_axis=0, concat_axis=0, tiled=True)]
    scatter x2 -> x0, local copies, waits for them, and re-layouts: 19.4 us -> none  [the longest x1 11.2 us: on_device(): jnp.zeros((owners_total * capacity, pixel_count), jnp.bfloat16)]
    all_to_all x9 -> x0, local copies, waits for them, and re-layouts: 14.3 us -> none  [the longest x1 3.79 us: on_device(): lax.all_to_all(lax.all_to_all(send_weights, 'grp', split_axis=0, concat_a...]
    reshape x10 -> x0, local copies, waits for them, and re-layouts: 10.1 us -> none  [the longest x2 8.65 us: on_device(): send_weights.reshape(group_count, sub_count, capacity, pixel_count)]
    dot_general x15 -> x1, matrix products: 7.29 us -> 0.2 us  [on_device(): part = jnp.dot(band, alm.reshape(freqs, 2 * L), preferred_element_type=F32)]
  transfers between devices with their start and end apart: 8 -> 0, of which waited for: 6 -> 0; matrix products, arithmetic and copies ran while one was open for 17% -> 0% of each run, Pallas kernels for 0% -> 0%
where the time goes in v1:
time: 90.4 us; the launch traced here: 89.9 us
  Pallas kernels  79.8 us (88%)
  local copies, waits for them, and re-layouts  8.79 us (10%)
  other arithmetic  1.09 us (1%)
    pallas_call x1, Pallas kernels, on_device(): pl.pallas_call(kernel, out_shape=jax.ShapeDtypeStruct((SD, HALF_DET), BF1...  79.8 us
    unnamed x13, local copies, waits for them, and re-layouts  7.2 us

profile of v1, /device:TPU:1, one launch (start us, length us, event | category | flops | bytes accessed | tf_op | source)
XLA Modules:
  0.0 89.9 jit_solution(15101515140200193106)
XLA Ops:
  0.0 1.2 %copy.12 = bf16[16,8,2,1024]{3,1,2,0:T(8,128)(2,1)S(1)} copy(bf16[16,8,2,1024]{3,2,1,0:T(2,128)(2,1)} %bitcast.10) | data formatting | bytes 1048576
  1.2 1.1 %select_reduce_fusion = bf16[32,128]{1,0:T(8,128)(2,1)S(1)} fusion(f32[32,32]{1,0:T(8,128)} %param.11, s32[128]{0:T(128)S(1)} %iota_add_fusion, s32[32,32]{1,0:T(8,128)} %param.10), kind=kLoop, calls=%fused_computation | loop fusion | flops 389120 | bytes 16896 | tf_op jit(solution)/shard_map/reduce_sum | solution.py:342
  2.3 0.2 fusion.2.part_ref
  2.5 0.8 broadcast_in_dim.2.ordb_ref
  3.3 0.0 copy-start
  3.3 1.6 %copy-done = bf16[1,1024,1024]{2,1,0:T(8,128)(2,1)S(1)} copy-done((bf16[1,1024,1024]{2,1,0:T(8,128)(2,1)S(1)}, bf16[1,1024,1024]{2,1,0:T(8,128)(2,1)}, u32[]{:S(2)}) %copy-start) | copy-done | bytes 2097176
  4.9 0.0 copy-start.1
  4.9 1.6 %copy-done.1 = bf16[2048,512]{1,0:T(8,128)(2,1)S(1)} copy-done((bf16[2048,512]{1,0:T(8,128)(2,1)S(1)}, bf16[2048,512]{1,0:T(8,128)(2,1)}, u32[]{:S(2)}) %copy-start.1) | copy-done | bytes 2097176
  6.4 0.0 copy-start.2
  6.4 0.8 copy-done.2
  7.2 0.0 copy-start.3
  7.2 0.7 copy-done.3
  7.9 0.0 copy-start.4
  7.9 0.7 copy-done.4
  8.6 0.0 copy-start.5
  8.6 0.7 copy-done.5
  9.3 79.8 %shard_map.91 = bf16[2048,16]{1,0:T(8,128)(2,1)S(1)} custom-call(s32[256]{0:T(256)S(1)} %copy-done.5, f32[32,2048]{1,0:T(8,128)S(1)} %fusion.2.part_ref, bf16[1,1024,1024]{2,1,0:T(8,128)(2,1)S(1)} %copy-done, bf16[2048,512]{1,0:T(8,128)(2,1)S(1)} %copy-done.1, s32[16,128]{1,0:T(8,128)S(1)} %bitcast.7, s32[16,128]{1,0:T(8,128)S(1)} %bitcast.8, ...), custom_call_target="tpu_custom_call" | custom-call | tf_op jit(solution)/shard_map/pallas_call | solution.py:353
  89.1 0.8 copy.11
  (1 shorter events, 0.0 us)
Async XLA Ops:
  3.3 1.6 %copy-start = (bf16[1,1024,1024]{2,1,0:T(8,128)(2,1)S(1)}, bf16[1,1024,1024]{2,1,0:T(8,128)(2,1)}, u32[]{:S(2)}) copy-start(bf16[1,1024,1024]{2,1,0:T(8,128)(2,1)} %leg_ref.1) | copy-start | bytes 6291460
  4.9 1.6 %copy-start.1 = (bf16[2048,512]{1,0:T(8,128)(2,1)S(1)}, bf16[2048,512]{1,0:T(8,128)(2,1)}, u32[]{:S(2)}) copy-start(bf16[2048,512]{1,0:T(8,128)(2,1)} %int_ref.1) | copy-start | bytes 6291460
  6.4 0.8 copy-start.2
  7.2 0.7 copy-start.3
  7.9 0.7 copy-start.4
  8.6 0.7 copy-start.5

commit v2 on v1

--- a/solution.py
+++ b/solution.py
@@ -47,18 +47,26 @@
 
 
 def kernel(
-    order_ref, part_ref, leg_ref, int_ref, own_ref, tile_ref, ordb_ref, tab_ref, out_ref,
-    part_s, part_r, leg_v, int_v, pick, d_s, d_r, y_s, y_r, y_f, coef, basis, acc, tiles,
+    alm_ref, bidx_hbm, bwt_hbm, leg_ref, ord_hbm, own_hbm, tile_hbm, int_ref, tab_hbm, out_ref,
+    bidx_ref, bwt_ref, ord_ref, own_ref, tile_ref, tab_ref, ordb_ref,
+    leg_v, int_v, pick, d_s, d_r, t_s, t_r, y_s, y_r, y_f, coef, basis, acc, tiles,
     v_s, v_r, cols, sel_v, sel_s, rank_v,
-    loc_sem, ex_sem, ys_sem, yr_sem, ds_sem, dr_sem, rs_sem, rr_sem, vs_sem, vr_sem,
+    loc_sem, ts_sem, tr_sem, ys_sem, yr_sem, ds_sem, dr_sem, rs_sem, rr_sem, vs_sem, vr_sem,
 ):
     f, z, s = lax.axis_index("freq"), lax.axis_index("grp"), lax.axis_index("sub")
     me = f * NS + s
 
-    leg_copy = pltpu.make_async_copy(
-        leg_ref.at[0, :, pl.ds(pl.multiple_of(f * RH, RH), RH)], leg_v, loc_sem.at[0]
-    )
+    leg_copy = pltpu.make_async_copy(leg_ref.at[0], leg_v, loc_sem.at[0])
     int_copy = pltpu.make_async_copy(int_ref, int_v, loc_sem.at[1])
+    small = [
+        pltpu.make_async_copy(source, target, loc_sem.at[2 + n])
+        for n, (source, target) in enumerate((
+            (bidx_hbm, bidx_ref), (bwt_hbm, bwt_ref), (ord_hbm, ord_ref),
+            (own_hbm, own_ref), (tile_hbm, tile_ref), (tab_hbm, tab_ref),
+        ))
+    ]
+    for copy in small:
+        copy.start()
     leg_copy.start()
     int_copy.start()
 
@@ -72,17 +80,56 @@
         return 0
 
     lax.fori_loop(1, NF * NS, greet, 0)
-    up, down = lax.rem(z + 1, NG), lax.rem(z + NG - 1, NG)
-    for zz in (up, down):
-        pl.semaphore_signal(barrier, inc=1, device_id=(f, zz, s), device_id_type=MESH)
-    part_s[...] = part_ref[...].astype(BF16)
-    pl.semaphore_wait(barrier, NF * NS - 1 + 2)
-
-    exchange = pltpu.make_async_remote_copy(
-        src_ref=part_s, dst_ref=part_r, send_sem=ex_sem.at[0], recv_sem=ex_sem.at[1],
-        device_id=(1 - f, z, s), device_id_type=MESH,
-    )
-    exchange.start()
+    for hops in (1, 2, NG - 2, NG - 1):
+        pl.semaphore_signal(
+            barrier, inc=1, device_id=(f, lax.rem(z + hops, NG), s), device_id_type=MESH
+        )
+
+    for copy in small:
+        copy.wait()
+    freqs = alm_ref.shape[0]
+    freq = lax.broadcasted_iota(I32, (DET, freqs), 1) + f * freqs
+    band = jnp.zeros((DET, freqs), F32)
+    for k in range(bidx_ref.shape[1]):
+        band = band + jnp.where(bidx_ref[:, k : k + 1] == freq, bwt_ref[:, k : k + 1], 0.0)
+    part = dot(band.astype(BF16), alm_ref[...])
+    for h in range(2):
+        spread_rows = jnp.broadcast_to(ord_ref[h : h + 1, :].astype(F32), (128, 128))
+        ordb_ref[h * 128 : (h + 1) * 128, :] = spread_rows.T.astype(I32)
+
+    degree = lax.rem(lax.broadcasted_iota(I32, (DET, 2 * L), 1), L)
+    order = ordb_ref[pl.ds(z * NS + s, 1), :][:, :1]
+    part = jnp.where(degree >= order, part, 0.0).astype(BF16)
+    leg_copy.wait()
+    cyc = dot(jnp.concatenate([part[:, :L], part[:, L:]], axis=0), leg_v[...])
+    turn = lax.broadcasted_iota(I32, (DET, RH), 1) & 3
+    quads = (
+        lax.broadcasted_iota(I32, (128, RH), 1) // 4 == lax.broadcasted_iota(I32, (128, RH), 0)
+    ).astype(BF16)
+    for h in range(NF):
+        pair = []
+        for c in range(2):
+            one = cyc[c * DET : (c + 1) * DET, h * RH : (h + 1) * RH]
+            spread = jnp.concatenate([jnp.where(turn == i, one, 0.0) for i in range(4)], axis=0)
+            pair.append(dot(quads, spread.astype(BF16), NT).reshape(NS, NJ, 128))
+        y_s[h] = jnp.concatenate(pair, axis=1).astype(BF16)
+
+    def y_copy(k, dst):
+        other = lax.rem(me + k, NF * NS)
+        oh, os = other // NS, lax.rem(other, NS)
+        return pltpu.make_async_remote_copy(
+            src_ref=y_s.at[oh, os], dst_ref=y_r.at[dst],
+            send_sem=ys_sem.at[k], recv_sem=yr_sem.at[k],
+            device_id=(oh, z, os), device_id_type=MESH,
+        )
+
+    def start_y(k, _):
+        y_copy(k, me).start()
+        return 0
+
+    pl.semaphore_wait(barrier, NF * NS - 1 + 4)
+    lax.fori_loop(1, NF * NS, start_y, 0)
+    y_r[me] = y_s[f, s]
 
     lane = lax.broadcasted_iota(I32, (128, 128), 1)
     row = lax.broadcasted_iota(I32, (128, 128), 0)
@@ -108,7 +155,7 @@
 
     def put_tiles(other, _):
         turned = pltpu.roll(half_tile, lax.rem(s - other + NS, NS) * NJ, 1)
-        y_s[other, 16:32, :] = jnp.where(mine16, turned, 0.0).astype(BF16)
+        t_s[other] = jnp.where(mine16, turned, 0.0).astype(BF16)
         return 0
 
     lax.fori_loop(0, NS, put_tiles, 0)
@@ -128,27 +175,10 @@
 
     lax.fori_loop(0, 4, pack, 0)
 
-    exchange.wait_recv()
-    total = part_ref[...] + part_r[...].astype(F32)
-    degree = lax.rem(lax.broadcasted_iota(I32, (DET, 2 * L), 1), L)
-    total = jnp.where(degree >= order_ref[z * NS + s], total, 0.0).astype(BF16)
-    leg_copy.wait()
-    cyc = dot(jnp.concatenate([total[:, :L], total[:, L:]], axis=0), leg_v[...])
-    turn = lax.broadcasted_iota(I32, (DET, RH), 1) & 3
-    quads = (
-        lax.broadcasted_iota(I32, (128, RH), 1) // 4 == lax.broadcasted_iota(I32, (128, RH), 0)
-    ).astype(BF16)
-    halves = []
-    for c in range(2):
-        one = cyc[c * DET : (c + 1) * DET, :]
-        spread = jnp.concatenate([jnp.where(turn == i, one, 0.0) for i in range(4)], axis=0)
-        halves.append(dot(quads, spread.astype(BF16), NT).reshape(NS, NJ, 128))
-    y_s[:, 0:16, :] = jnp.concatenate(halves, axis=1).astype(BF16)
-
-    def y_copy(k, dst):
+    def t_copy(k, dst):
         return pltpu.make_async_remote_copy(
-            src_ref=y_s.at[lax.rem(s + k, NS)], dst_ref=y_r.at[dst],
-            send_sem=ys_sem.at[k], recv_sem=yr_sem.at[k],
+            src_ref=t_s.at[lax.rem(s + k, NS)], dst_ref=t_r.at[dst],
+            send_sem=ts_sem.at[k], recv_sem=tr_sem.at[k],
             device_id=(f, z, lax.rem(s + k, NS)), device_id_type=MESH,
         )
 
@@ -159,18 +189,61 @@
             device_id=(f, z, lax.rem(s + k, NS)), device_id_type=MESH,
         )
 
-    def start_y(k, _):
-        y_copy(k, s).start()
-        return 0
-
     def start_d(k, _):
+        t_copy(k, s).start()
         d_copy(k, s).start()
         return 0
 
-    lax.fori_loop(1, NS, start_y, 0)
     lax.fori_loop(1, NS, start_d, 0)
-    y_r[s] = y_s[s]
+    t_r[s] = t_s[s]
     d_r[s] = d_s[s]
+
+    def wait_y(k, _):
+        y_copy(k, lax.rem(me + NF * NS - k, NF * NS)).wait_recv()
+        return 0
+
+    lax.fori_loop(1, NF * NS, wait_y, 0)
+    y_f[...] = (y_r[0:NS].astype(F32) + y_r[NS : 2 * NS].astype(F32)).reshape(NS * 16, 128)
+    for c in range(2):
+        for j in range(NJ):
+            coef[c * 16 : (c + 1) * 16, j * 128 : (j + 1) * 128] = y_f[
+                pl.ds(c * NJ + j, NS, stride=16), :
+            ].astype(BF16)
+
+    def slot(d, way):
+        return 0 if d == 0 else 2 * d - (way == 0)
+
+    def ring(d, hops, way, c):
+        source, target = slot(d, way) * 32 + c * 16, slot(d + hops, way) * 32 + c * 16
+        sem = slot(d + hops, way) * 2 + c
+        return pltpu.make_async_remote_copy(
+            src_ref=coef.at[pl.ds(source, 16), :], dst_ref=coef.at[pl.ds(target, 16), :],
+            send_sem=rs_sem.at[sem], recv_sem=rr_sem.at[sem],
+            device_id=(f, lax.rem(z + (hops if way == 0 else NG - hops), NG), s), device_id_type=MESH,
+        )
+
+    def ring_step(d):
+        for hops in (2, 1):
+            for c in range(2):
+                for way in range(2):
+                    if d > 0 and hops == 2:
+                        ring(d - 2, 2, way, c).wait_recv()
+                    if d + hops < 8 or way == 0:
+                        ring(d, hops, way, c).start()
+
+    def ring_wait(*steps):
+        for d, hops in steps:
+            for c in range(2):
+                for way in range(2):
+                    if d + hops < 8 or way == 0:
+                        ring(d, hops, way, c).wait_recv()
+
+    def sky_first(j, _):
+        at = pl.multiple_of(j * 128, 128)
+        acc[pl.ds(at, 128), :] = dot(coef[0:256, pl.ds(at, 128)], basis[0:256, :], TN)
+        return 0
+
+    ring_step(0)
 
     def make_basis(p, _):
         hops = (p + 1) // 2
@@ -200,40 +273,13 @@
     for c in range(SD // 128):
         sel_v[c * 128 : (c + 1) * 128, :] = (place == turned_cols[:, c : c + 1]).astype(BF16)
 
-    def wait_y(k, _):
-        y_copy(k, lax.rem(s + NS - k, NS)).wait_recv()
-        return 0
-
-    lax.fori_loop(1, NS, wait_y, 0)
-    y_f[...] = y_r[:, 0:16, :].astype(F32).reshape(NS * 16, 128)
-    for c in range(2):
-        for j in range(NJ):
-            coef[c * 16 : (c + 1) * 16, j * 128 : (j + 1) * 128] = y_f[
-                pl.ds(c * NJ + j, NS, stride=16), :
-            ].astype(BF16)
-
-    def ring(k, way):
-        source = 0 if k == 1 else 2 * (k - 1) - (way == 0)
-        target = 2 * k - (way == 0)
-        return pltpu.make_async_remote_copy(
-            src_ref=coef.at[pl.ds(source * 32, 32), :], dst_ref=coef.at[pl.ds(target * 32, 32), :],
-            send_sem=rs_sem.at[target], recv_sem=rr_sem.at[target],
-            device_id=(f, up if way == 0 else down, s), device_id_type=MESH,
-        )
-
-    def sky_first(j, _):
-        at = pl.multiple_of(j * 128, 128)
-        acc[pl.ds(at, 128), :] = dot(coef[0:256, pl.ds(at, 128)], basis[0:256, :], TN)
-        return 0
-
-    for k in range(1, 9):
-        ways = (0, 1) if k < 8 else (0,)
-        for way in ways:
-            ring(k, way).start()
-        if k >= 5:
-            lax.fori_loop((k - 5) * 2, (k - 4) * 2, sky_first, 0)
-        for way in ways:
-            ring(k, way).wait_recv()
+    ring_step(2)
+    ring_step(4)
+    ring_wait((0, 1), (2, 1))
+    lax.fori_loop(0, 4, sky_first, 0)
+    ring_step(6)
+    lax.fori_loop(4, 8, sky_first, 0)
+    ring_wait((4, 1), (6, 2), (6, 1))
 
     def sky_last(j, _):
         at = pl.multiple_of(j * 128, 128)
@@ -248,7 +294,12 @@
 
     lax.fori_loop(0, NJ, sky_last, 0)
 
-    tile_sum = jnp.sum(y_r[:, 16:32, :].astype(F32), axis=0).astype(BF16)
+    def wait_t(k, _):
+        t_copy(k, lax.rem(s + NS - k, NS)).wait_recv()
+        return 0
+
+    lax.fori_loop(1, NS, wait_t, 0)
+    tile_sum = jnp.sum(t_r[...].astype(F32), axis=0).astype(BF16)
     here = (lax.broadcasted_iota(I32, (128, LANES), 0) == tab_ref[0:1, :]).astype(BF16)
     by_rank = dot(tile_sum, here)
     own_rank = lax.broadcasted_iota(I32, (16, LANES), 0) == tab_ref[1:2, :]
@@ -310,63 +361,60 @@
     lax.fori_loop(1, NF * NS, wait_v, 0)
 
     found = dot(sel_v[...], v_r[...].reshape(NF * NS * 16, 128))
-    fold = ((row & (HALF_DET - 1)) == lane).astype(BF16)
+    fold = (rank_row == (lane16 & (HALF_DET - 1))).astype(BF16)
     lane_band = (lane // HALF_DET).astype(F32)
     for c in range(SD // 128):
         kept = jnp.where(
             lane_band == turned_cols[:, 16 + c : 17 + c], found[c * 128 : (c + 1) * 128, :], 0.0
         )
-        out_ref[c * 128 : (c + 1) * 128, :] = dot(kept.astype(BF16), fold)[:, :HALF_DET].astype(BF16)
-
-    exchange.wait_send()
+        out_ref[:, c * 128 : (c + 1) * 128] = dot(fold, kept.astype(BF16), NT).astype(BF16)
 
     def sent(k, _):
-        y_copy(k, s).wait_send()
+        t_copy(k, s).wait_send()
         d_copy(k, s).wait_send()
         return 0
 
-    def sent_v(k, _):
+    def sent_all(k, _):
+        y_copy(k, me).wait_send()
         v_copy(k, me).wait_send()
         return 0
 
     lax.fori_loop(1, NS, sent, 0)
-    lax.fori_loop(1, NF * NS, sent_v, 0)
-    for k in range(1, 9):
-        for way in (0, 1) if k < 8 else (0,):
-            ring(k, way).wait_send()
-
-
-def band_matrix(band_index, band_weight, first_freq, freq_count):
-    freq_ids = first_freq + lax.iota(I32, freq_count)
-    matches = (band_index[:, :, None] == freq_ids[None, None, :]).astype(F32)
-    return jnp.sum(matches * band_weight[:, :, None], axis=1).astype(BF16)
+    lax.fori_loop(1, NF * NS, sent_all, 0)
+    for d in range(0, 8, 2):
+        for hops in (1, 2):
+            for c in range(2):
+                for way in range(2):
+                    if d + hops < 8 or way == 0:
+                        ring(d, hops, way, c).wait_send()
 
 
 def on_device(alm, band_index, band_weight, legendre, orders, owner, tile_local, interp):
-    freqs = alm.shape[0]
-    band = band_matrix(band_index, band_weight, lax.axis_index("freq") * freqs, freqs)
-    part = jnp.dot(band, alm.reshape(freqs, 2 * L), preferred_element_type=F32)
-    order_rows = jnp.broadcast_to(orders[:, None], (orders.shape[0], 128))
     dma = pltpu.SemaphoreType.DMA
     vmem = pl.BlockSpec(memory_space=pltpu.VMEM)
-    anywhere = pl.BlockSpec(memory_space=pl.ANY)
-    return pl.pallas_call(
+    hbm = pl.BlockSpec(memory_space=pltpu.HBM)
+    turned = pl.pallas_call(
         kernel,
-        out_shape=jax.ShapeDtypeStruct((SD, HALF_DET), BF16),
-        in_specs=[
-            pl.BlockSpec(memory_space=pltpu.SMEM), vmem, anywhere, anywhere, vmem, vmem, vmem, vmem,
-        ],
+        out_shape=jax.ShapeDtypeStruct((HALF_DET, SD), BF16),
+        in_specs=[vmem] + [hbm] * 8,
         out_specs=vmem,
         scratch_shapes=[
-            pltpu.VMEM((DET, 2 * L), BF16),
-            pltpu.VMEM((DET, 2 * L), BF16),
-            pltpu.VMEM((L, RH), BF16),
+            pltpu.VMEM(band_index.shape, I32),
+            pltpu.VMEM(band_weight.shape, F32),
+            pltpu.VMEM((2, 128), I32),
+            pltpu.VMEM((16, 128), I32),
+            pltpu.VMEM((16, 128), I32),
+            pltpu.VMEM((8, LANES), I32),
+            pltpu.VMEM((256, 128), I32),
+            pltpu.VMEM(legendre.shape[1:], BF16),
             pltpu.VMEM((SD, PIX), BF16),
             pltpu.VMEM((4 * ROWS, SD), BF16),
             pltpu.VMEM((NS, ROWS, PIX), BF16),
             pltpu.VMEM((NS, ROWS, PIX), BF16),
-            pltpu.VMEM((NS, 32, 128), BF16),
-            pltpu.VMEM((NS, 32, 128), BF16),
+            pltpu.VMEM((NS, 16, 128), BF16),
+            pltpu.VMEM((NS, 16, 128), BF16),
+            pltpu.VMEM((NF, NS, 16, 128), BF16),
+            pltpu.VMEM((NF * NS, 16, 128), BF16),
             pltpu.VMEM((NS * 16, 128), F32),
             pltpu.VMEM((NG * 32, 1024), BF16),
             pltpu.VMEM((NG * 32, NPHI), BF16),
@@ -378,16 +426,17 @@
             pltpu.VMEM((SD, NF * NS * 16), BF16),
             pltpu.VMEM((256, LANES), BF16),
             pltpu.VMEM((16, 128), I32),
-            dma((2,)), dma((2,)), dma((NS,)), dma((NS,)), dma((NS,)), dma((NS,)),
-            dma((NG,)), dma((NG,)), dma((NF * NS,)), dma((NF * NS,)),
+            dma((8,)), dma((NS,)), dma((NS,)), dma((NF * NS,)), dma((NF * NS,)), dma((NS,)), dma((NS,)),
+            dma((2 * NG,)), dma((2 * NG,)), dma((NF * NS,)), dma((NF * NS,)),
         ],
         compiler_params=pltpu.CompilerParams(
-            collective_id=0, has_side_effects=True, vmem_limit_bytes=48 * 2**20
+            collective_id=0, has_side_effects=True, vmem_limit_bytes=65_500_000
         ),
     )(
-        orders, part, legendre, interp, owner.reshape(16, 128), tile_local.reshape(16, 128),
-        order_rows, jnp.asarray(lane_table()),
+        alm.reshape(alm.shape[0], 2 * L), band_index, band_weight, legendre, orders.reshape(2, 128),
+        owner.reshape(16, 128), tile_local.reshape(16, 128), interp, jnp.asarray(lane_table()),
     )
+    return turned.T
 
 
 def solution(mesh):

time: 90.4 us -> 62 us (0.69)
  Pallas kernels: 79.8 us -> 58.3 us
  local copies, waits for them, and re-layouts: 8.79 us -> 3.43 us
  other arithmetic: 1.09 us -> 0 us
    pallas_call x1, Pallas kernels: 79.8 us -> 58.3 us  [on_device(): pl.pallas_call(kernel, out_shape=jax.ShapeDtypeStruct((HALF_DET, SD), BF1...]
    unnamed x13 -> x2, local copies, waits for them, and re-layouts: 7.2 us -> 3.43 us
    reduce_sum x1 -> x0, other arithmetic: 1.09 us -> none  [band_matrix(): return jnp.sum(matches * band_weight[:, :, None], axis=1).astype(BF16)]
where the time goes in v2:
time: 62 us; the launch traced here: 61.8 us
  Pallas kernels  58.3 us (94%)
  local copies, waits for them, and re-layouts  3.43 us (6%)
    pallas_call x1, Pallas kernels, on_device(): pl.pallas_call(kernel, out_shape=jax.ShapeDtypeStruct((HALF_DET, SD), BF1...  58.3 us
    unnamed x2, local copies, waits for them, and re-layouts  3.43 us

profile of v2, /device:TPU:1, one launch (start us, length us, event | category | flops | bytes accessed | tf_op | source)
XLA Modules:
  0.0 61.8 jit_solution(17528813934475377556)
XLA Ops:
  0.0 2.0 %copy.10 = bf16[16,8,2,1024]{3,1,2,0:T(8,128)(2,1)} copy(bf16[16,8,2,1024]{3,2,1,0:T(2,128)(2,1)} %bitcast.8) | data formatting | bytes 1048576
  2.0 58.3 %shard_map.91 = bf16[16,2048]{1,0:T(8,128)(2,1)} custom-call(bf16[128,2048]{1,0:T(8,128)(2,1)} %bitcast.7, s32[32,32]{1,0:T(8,128)} %bidx_hbm.1, f32[32,32]{1,0:T(8,128)} %bwt_hbm.1, bf16[1,1024,1024]{2,1,0:T(8,128)(2,1)} %leg_ref.1, s32[2,128]{1,0:T(2,128)} %bitcast.12, s32[16,128]{1,0:T(8,128)} %bitcast.10, s32[16,128]{1,0:T(8,128)} %bitcast.11, ...), custom_call_target="tpu_custom_call" | custom-call | tf_op jit(solution)/shard_map/pallas_call | solution.py:396
  60.3 1.5 %copy.12 = bf16[2048,16]{0,1:T(8,128)(2,1)} copy(bf16[2048,16]{0,1:T(8,128)(2,1)} %bitcast.9) | data formatting | bytes 131072

commit v3 on v2

--- a/solution.py
+++ b/solution.py
@@ -47,9 +47,9 @@
 
 
 def kernel(
-    alm_ref, bidx_hbm, bwt_hbm, leg_ref, ord_hbm, own_hbm, tile_hbm, int_ref, tab_hbm, out_ref,
-    bidx_ref, bwt_ref, ord_ref, own_ref, tile_ref, tab_ref, ordb_ref,
-    leg_v, int_v, pick, d_s, d_r, t_s, t_r, y_s, y_r, y_f, coef, basis, acc, tiles,
+    alm_hbm, bidx_hbm, bwt_hbm, leg_ref, ord_hbm, own_hbm, tile_hbm, int_ref, tab_hbm, out_ref,
+    alm_ref, bidx_ref, bwt_ref, ord_ref, own_ref, tile_ref, tab_ref, ordb_ref,
+    leg_v, int_v, pick, d_s, d_r, t_s, t_r, y_s, y_r, y_f, coef, coef_t, basis, acc, tiles,
     v_s, v_r, cols, sel_v, sel_s, rank_v,
     loc_sem, ts_sem, tr_sem, ys_sem, yr_sem, ds_sem, dr_sem, rs_sem, rr_sem, vs_sem, vr_sem,
 ):
@@ -61,7 +61,7 @@
     small = [
         pltpu.make_async_copy(source, target, loc_sem.at[2 + n])
         for n, (source, target) in enumerate((
-            (bidx_hbm, bidx_ref), (bwt_hbm, bwt_ref), (ord_hbm, ord_ref),
+            (alm_hbm, alm_ref), (bidx_hbm, bidx_ref), (bwt_hbm, bwt_ref), (ord_hbm, ord_ref),
             (own_hbm, own_ref), (tile_hbm, tile_ref), (tab_hbm, tab_ref),
         ))
     ]
@@ -92,7 +92,8 @@
     band = jnp.zeros((DET, freqs), F32)
     for k in range(bidx_ref.shape[1]):
         band = band + jnp.where(bidx_ref[:, k : k + 1] == freq, bwt_ref[:, k : k + 1], 0.0)
-    part = dot(band.astype(BF16), alm_ref[...])
+    band = band.astype(BF16)
+    part = jnp.concatenate([dot(band, alm_ref[:, c, :]) for c in range(2)], axis=1)
     for h in range(2):
         spread_rows = jnp.broadcast_to(ord_ref[h : h + 1, :].astype(F32), (128, 128))
         ordb_ref[h * 128 : (h + 1) * 128, :] = spread_rows.T.astype(I32)
@@ -211,7 +212,7 @@
             ].astype(BF16)
 
     def slot(d, way):
-        return 0 if d == 0 else 2 * d - (way == 0)
+        return 0 if d == 0 else min(2 * d - (way == 0), NG - 1)
 
     def ring(d, hops, way, c):
         source, target = slot(d, way) * 32 + c * 16, slot(d + hops, way) * 32 + c * 16
@@ -228,19 +229,19 @@
                 for way in range(2):
                     if d > 0 and hops == 2:
                         ring(d - 2, 2, way, c).wait_recv()
-                    if d + hops < 8 or way == 0:
+                    if d + hops < 8 or way == c:
                         ring(d, hops, way, c).start()
 
     def ring_wait(*steps):
         for d, hops in steps:
             for c in range(2):
                 for way in range(2):
-                    if d + hops < 8 or way == 0:
+                    if d + hops < 8 or way == c:
                         ring(d, hops, way, c).wait_recv()
 
-    def sky_first(j, _):
-        at = pl.multiple_of(j * 128, 128)
-        acc[pl.ds(at, 128), :] = dot(coef[0:256, pl.ds(at, 128)], basis[0:256, :], TN)
+    def sky_first(n, _):
+        at = pl.ds(pl.multiple_of(n * 256, 256), 256)
+        acc[:, at] = dot(coef_t[...], basis[0:256, at])
         return 0
 
     ring_step(0)
@@ -276,23 +277,27 @@
     ring_step(2)
     ring_step(4)
     ring_wait((0, 1), (2, 1))
-    lax.fori_loop(0, 4, sky_first, 0)
+    coef_t[...] = coef[0:256, :].T
+    lax.fori_loop(0, 2, sky_first, 0)
     ring_step(6)
-    lax.fori_loop(4, 8, sky_first, 0)
+    lax.fori_loop(2, 4, sky_first, 0)
     ring_wait((4, 1), (6, 2), (6, 1))
 
-    def sky_last(j, _):
-        at = pl.multiple_of(j * 128, 128)
-        sky = acc[pl.ds(at, 128), :] + dot(coef[256:512, pl.ds(at, 128)], basis[256:512, :], TN)
-        sky = sky.astype(BF16)
-        for i in range(4):
-            for t in range(8):
-                tiles[j, t * DET : (t + 1) * DET, i * 128 : (i + 1) * 128] = sky[
-                    i * DET : (i + 1) * DET, t * 128 : (t + 1) * 128
-                ]
-        return 0
-
-    lax.fori_loop(0, NJ, sky_last, 0)
+    def sky_last(n, _):
+        at = pl.ds(pl.multiple_of(n * 256, 256), 256)
+        sky = (acc[:, at] + dot(coef_t[...], basis[256:512, at])).astype(BF16)
+        for h in range(2):
+            to = pl.ds(pl.multiple_of((2 * n + h) * DET, DET), DET)
+            for j in range(NJ):
+                for i in range(4):
+                    top = j * 128 + i * DET
+                    tiles[j, to, i * 128 : (i + 1) * 128] = sky[
+                        top : top + DET, h * 128 : (h + 1) * 128
+                    ]
+        return 0
+
+    coef_t[...] = coef[256:512, :].T
+    lax.fori_loop(0, 4, sky_last, 0)
 
     def wait_t(k, _):
         t_copy(k, lax.rem(s + NS - k, NS)).wait_recv()
@@ -314,17 +319,14 @@
     sums = []
     for g in range(2):
         weights = d_r[:, g * GROUP : (g + 1) * GROUP, :].reshape(HALF_LANES, PIX)
-        picked = code[:, g * HALF_LANES : (g + 1) * HALF_LANES]
-
-        def one_band(j, value, g=g, weights=weights, picked=picked):
-            every = dot(tiles[g * 4 + j], weights, NT)
-            for t in range(8):
-                value = value + jnp.where(
-                    picked == j * 8 + t, every[t * DET : (t + 1) * DET, :], 0.0
-                )
-            return value
-
-        sums.append(lax.fori_loop(0, 4, one_band, jnp.zeros((DET, HALF_LANES), F32)))
+        pixels = tiles[g * 4 : (g + 1) * 4].reshape(4 * 8 * DET, PIX)
+        for n in range(HALF_LANES // 256):
+            every = dot(pixels, weights[n * 256 : (n + 1) * 256, :], NT)
+            picked = code[:, g * HALF_LANES + n * 256 : g * HALF_LANES + (n + 1) * 256]
+            value = jnp.zeros((DET, 256), F32)
+            for t in range(32):
+                value = value + jnp.where(picked == t, every[t * DET : (t + 1) * DET, :], 0.0)
+            sums.append(value)
     value = jnp.concatenate(sums, axis=1)
     band = tab_ref[2:3, :]
     spread = jnp.concatenate(
@@ -385,7 +387,7 @@
         for hops in (1, 2):
             for c in range(2):
                 for way in range(2):
-                    if d + hops < 8 or way == 0:
+                    if d + hops < 8 or way == c:
                         ring(d, hops, way, c).wait_send()
 
 
@@ -396,9 +398,10 @@
     turned = pl.pallas_call(
         kernel,
         out_shape=jax.ShapeDtypeStruct((HALF_DET, SD), BF16),
-        in_specs=[vmem] + [hbm] * 8,
+        in_specs=[hbm] * 9,
         out_specs=vmem,
         scratch_shapes=[
+            pltpu.VMEM((alm.shape[0], 2, L), BF16),
             pltpu.VMEM(band_index.shape, I32),
             pltpu.VMEM(band_weight.shape, F32),
             pltpu.VMEM((2, 128), I32),
@@ -417,6 +420,7 @@
             pltpu.VMEM((NF * NS, 16, 128), BF16),
             pltpu.VMEM((NS * 16, 128), F32),
             pltpu.VMEM((NG * 32, 1024), BF16),
+            pltpu.VMEM((1024, 256), BF16),
             pltpu.VMEM((NG * 32, NPHI), BF16),
             pltpu.VMEM((1024, NPHI), F32),
             pltpu.VMEM((NJ, 8 * DET, PIX), BF16),
@@ -426,14 +430,14 @@
             pltpu.VMEM((SD, NF * NS * 16), BF16),
             pltpu.VMEM((256, LANES), BF16),
             pltpu.VMEM((16, 128), I32),
-            dma((8,)), dma((NS,)), dma((NS,)), dma((NF * NS,)), dma((NF * NS,)), dma((NS,)), dma((NS,)),
+            dma((9,)), dma((NS,)), dma((NS,)), dma((NF * NS,)), dma((NF * NS,)), dma((NS,)), dma((NS,)),
             dma((2 * NG,)), dma((2 * NG,)), dma((NF * NS,)), dma((NF * NS,)),
         ],
         compiler_params=pltpu.CompilerParams(
             collective_id=0, has_side_effects=True, vmem_limit_bytes=65_500_000
         ),
     )(
-        alm.reshape(alm.shape[0], 2 * L), band_index, band_weight, legendre, orders.reshape(2, 128),
+        alm.reshape(alm.shape[0], 2, L), band_index, band_weight, legendre, orders.reshape(2, 128),
         owner.reshape(16, 128), tile_local.reshape(16, 128), interp, jnp.asarray(lane_table()),
     )
     return turned.T

time: 62 us -> 57.9 us (0.934)
  Pallas kernels: 58.3 us -> 56.2 us
  local copies, waits for them, and re-layouts: 3.43 us -> 1.47 us
    pallas_call x1, Pallas kernels: 58.3 us -> 56.2 us  [on_device(): pl.pallas_call(kernel, out_shape=jax.ShapeDtypeStruct((HALF_DET, SD), BF1...]
    unnamed x2 -> x1, local copies, waits for them, and re-layouts: 3.43 us -> 1.47 us
where the time goes in v3:
time: 57.9 us; the launch traced here: 57.7 us
  Pallas kernels  56.2 us (97%)
  local copies, waits for them, and re-layouts  1.47 us (3%)
    pallas_call x1, Pallas kernels, on_device(): pl.pallas_call(kernel, out_shape=jax.ShapeDtypeStruct((HALF_DET, SD), BF1...  56.2 us
    unnamed x1, local copies, waits for them, and re-layouts  1.47 us

profile of v3, /device:TPU:1, one launch (start us, length us, event | category | flops | bytes accessed | tf_op | source)
XLA Modules:
  0.0 57.7 jit_solution(5263267070747064726)
XLA Ops:
  0.0 56.2 %shard_map.91 = bf16[16,2048]{1,0:T(8,128)(2,1)} custom-call(bf16[128,2,1024]{2,1,0:T(2,128)(2,1)} %bitcast.5, s32[32,32]{1,0:T(8,128)} %bidx_hbm.1, f32[32,32]{1,0:T(8,128)} %bwt_hbm.1, bf16[1,1024,1024]{2,1,0:T(8,128)(2,1)} %leg_ref.1, s32[2,128]{1,0:T(2,128)} %bitcast.9, s32[16,128]{1,0:T(8,128)} %bitcast.7, s32[16,128]{1,0:T(8,128)} %bitcast.8, ...), custom_call_target="tpu_custom_call" | custom-call | tf_op jit(solution)/shard_map/pallas_call | solution.py:398
  56.3 1.5 %copy.11 = bf16[2048,16]{0,1:T(8,128)(2,1)} copy(bf16[2048,16]{0,1:T(8,128)(2,1)} %bitcast.6) | data formatting | bytes 131072

commit v4 on v3

--- a/solution.py
+++ b/solution.py
@@ -161,41 +161,43 @@
 
     lax.fori_loop(0, NS, put_tiles, 0)
 
+    def t_copy(k, dst):
+        return pltpu.make_async_remote_copy(
+            src_ref=t_s.at[lax.rem(s + k, NS)], dst_ref=t_r.at[dst],
+            send_sem=ts_sem.at[k], recv_sem=tr_sem.at[k],
+            device_id=(f, z, lax.rem(s + k, NS)), device_id_type=MESH,
+        )
+
+    def d_copy(k, dst):
+        return pltpu.make_async_remote_copy(
+            src_ref=d_s.at[lax.rem(s + k, NS)], dst_ref=d_r.at[dst],
+            send_sem=ds_sem.at[k], recv_sem=dr_sem.at[k],
+            device_id=(f, z, lax.rem(s + k, NS)), device_id_type=MESH,
+        )
+
     int_copy.wait()
-    slot_row = lax.broadcasted_iota(I32, (4 * ROWS, 128), 0)
+    slot_row = lax.broadcasted_iota(I32, (ROWS, 128), 0)
 
     def pack(q, _):
-        wanted = slot_row + q * (4 * ROWS)
+        wanted = jnp.concatenate(
+            [slot_row + lax.rem(s + q * 4 + n, NS) * ROWS for n in range(4)], axis=0
+        )
         for c in range(SD // 128):
             key = (own_ref[c : c + 1, :] - f * 128) * CAP + rank_v[c : c + 1, :]
             pick[:, c * 128 : (c + 1) * 128] = jnp.where(wanted == key, 1.0, 0.0).astype(BF16)
         packed = dot(pick[...], int_v[...]).astype(BF16)
         for n in range(4):
-            d_s[q * 4 + n] = packed[n * ROWS : (n + 1) * ROWS, :]
-        return 0
-
-    lax.fori_loop(0, 4, pack, 0)
-
-    def t_copy(k, dst):
-        return pltpu.make_async_remote_copy(
-            src_ref=t_s.at[lax.rem(s + k, NS)], dst_ref=t_r.at[dst],
-            send_sem=ts_sem.at[k], recv_sem=tr_sem.at[k],
-            device_id=(f, z, lax.rem(s + k, NS)), device_id_type=MESH,
-        )
-
-    def d_copy(k, dst):
-        return pltpu.make_async_remote_copy(
-            src_ref=d_s.at[lax.rem(s + k, NS)], dst_ref=d_r.at[dst],
-            send_sem=ds_sem.at[k], recv_sem=dr_sem.at[k],
-            device_id=(f, z, lax.rem(s + k, NS)), device_id_type=MESH,
-        )
-
-    def start_d(k, _):
-        t_copy(k, s).start()
-        d_copy(k, s).start()
-        return 0
-
-    lax.fori_loop(1, NS, start_d, 0)
+            k = q * 4 + n
+            d_s[lax.rem(s + k, NS)] = packed[n * ROWS : (n + 1) * ROWS, :]
+
+            @pl.when(k > 0)
+            def _(k=k):
+                t_copy(k, s).start()
+                d_copy(k, s).start()
+
+        return 0
+
+    lax.fori_loop(0, 2, pack, 0)
     t_r[s] = t_s[s]
     d_r[s] = d_s[s]
 
@@ -245,6 +247,7 @@
         return 0
 
     ring_step(0)
+    lax.fori_loop(2, 4, pack, 0)
 
     def make_basis(p, _):
         hops = (p + 1) // 2

time: 57.9 us -> 57 us (0.984)
  Pallas kernels: 56.2 us -> 55.4 us
    pallas_call x1, Pallas kernels: 56.2 us -> 55.4 us  [on_device(): pl.pallas_call(kernel, out_shape=jax.ShapeDtypeStruct((HALF_DET, SD), BF1...]
where the time goes in v4:
time: 57 us; the launch traced here: 56.9 us
  Pallas kernels  55.4 us (97%)
  local copies, waits for them, and re-layouts  1.47 us (3%)
    pallas_call x1, Pallas kernels, on_device(): pl.pallas_call(kernel, out_shape=jax.ShapeDtypeStruct((HALF_DET, SD), BF1...  55.4 us
    unnamed x1, local copies, waits for them, and re-layouts  1.47 us

profile of v4, /device:TPU:1, one launch (start us, length us, event | category | flops | bytes accessed | tf_op | source)
XLA Modules:
  0.0 56.9 jit_solution(214881348310796949)
XLA Ops:
  0.0 55.4 %shard_map.91 = bf16[16,2048]{1,0:T(8,128)(2,1)} custom-call(bf16[128,2,1024]{2,1,0:T(2,128)(2,1)} %bitcast.5, s32[32,32]{1,0:T(8,128)} %bidx_hbm.1, f32[32,32]{1,0:T(8,128)} %bwt_hbm.1, bf16[1,1024,1024]{2,1,0:T(8,128)(2,1)} %leg_ref.1, s32[2,128]{1,0:T(2,128)} %bitcast.9, s32[16,128]{1,0:T(8,128)} %bitcast.7, s32[16,128]{1,0:T(8,128)} %bitcast.8, ...), custom_call_target="tpu_custom_call" | custom-call | tf_op jit(solution)/shard_map/pallas_call | solution.py:401
  55.4 1.5 %copy.11 = bf16[2048,16]{0,1:T(8,128)(2,1)} copy(bf16[2048,16]{0,1:T(8,128)(2,1)} %bitcast.6) | data formatting | bytes 131072

commit v5 on v4

--- a/solution.py
+++ b/solution.py
@@ -284,7 +284,22 @@
     lax.fori_loop(0, 2, sky_first, 0)
     ring_step(6)
     lax.fori_loop(2, 4, sky_first, 0)
-    ring_wait((4, 1), (6, 2), (6, 1))
+    ring_wait((4, 1))
+    coef_t[:, 0:128] = coef[256:384, :].T
+
+    def wait_t(k, _):
+        t_copy(k, lax.rem(s + NS - k, NS)).wait_recv()
+        return 0
+
+    lax.fori_loop(1, NS, wait_t, 0)
+    tile_sum = jnp.sum(t_r[...].astype(F32), axis=0).astype(BF16)
+    here = (lax.broadcasted_iota(I32, (128, LANES), 0) == tab_ref[0:1, :]).astype(BF16)
+    by_rank = dot(tile_sum, here)
+    own_rank = lax.broadcasted_iota(I32, (16, LANES), 0) == tab_ref[1:2, :]
+    code = jnp.sum(jnp.where(own_rank, by_rank, 0.0), axis=0, keepdims=True).astype(I32)
+    code = code + tab_ref[4:5, :]
+
+    ring_wait((6, 2), (6, 1))
 
     def sky_last(n, _):
         at = pl.ds(pl.multiple_of(n * 256, 256), 256)
@@ -299,20 +314,8 @@
                     ]
         return 0
 
-    coef_t[...] = coef[256:512, :].T
+    coef_t[:, 128:256] = coef[384:512, :].T
     lax.fori_loop(0, 4, sky_last, 0)
-
-    def wait_t(k, _):
-        t_copy(k, lax.rem(s + NS - k, NS)).wait_recv()
-        return 0
-
-    lax.fori_loop(1, NS, wait_t, 0)
-    tile_sum = jnp.sum(t_r[...].astype(F32), axis=0).astype(BF16)
-    here = (lax.broadcasted_iota(I32, (128, LANES), 0) == tab_ref[0:1, :]).astype(BF16)
-    by_rank = dot(tile_sum, here)
-    own_rank = lax.broadcasted_iota(I32, (16, LANES), 0) == tab_ref[1:2, :]
-    code = jnp.sum(jnp.where(own_rank, by_rank, 0.0), axis=0, keepdims=True).astype(I32)
-    code = code + tab_ref[4:5, :]
 
     def wait_d(k, _):
         d_copy(k, lax.rem(s + NS - k, NS)).wait_recv()

time: 57 us -> 56.7 us (level)
  no operation moved by 1% of the time
where the time goes in v5:
time: 56.7 us; the launch traced here: 56.5 us
  Pallas kernels  55.1 us (97%)
  local copies, waits for them, and re-layouts  1.47 us (3%)
    pallas_call x1, Pallas kernels, on_device(): pl.pallas_call(kernel, out_shape=jax.ShapeDtypeStruct((HALF_DET, SD), BF1...  55.1 us
    unnamed x1, local copies, waits for them, and re-layouts  1.47 us

profile of v5, /device:TPU:1, one launch (start us, length us, event | category | flops | bytes accessed | tf_op | source)
XLA Modules:
  0.0 56.5 jit_solution(2497859106939662583)
XLA Ops:
  0.0 55.1 %shard_map.91 = bf16[16,2048]{1,0:T(8,128)(2,1)} custom-call(bf16[128,2,1024]{2,1,0:T(2,128)(2,1)} %bitcast.5, s32[32,32]{1,0:T(8,128)} %bidx_hbm.1, f32[32,32]{1,0:T(8,128)} %bwt_hbm.1, bf16[1,1024,1024]{2,1,0:T(8,128)(2,1)} %leg_ref.1, s32[2,128]{1,0:T(2,128)} %bitcast.9, s32[16,128]{1,0:T(8,128)} %bitcast.7, s32[16,128]{1,0:T(8,128)} %bitcast.8, ...), custom_call_target="tpu_custom_call" | custom-call | tf_op jit(solution)/shard_map/pallas_call | solution.py:404
  55.1 1.5 %copy.11 = bf16[2048,16]{0,1:T(8,128)(2,1)} copy(bf16[2048,16]{0,1:T(8,128)(2,1)} %bitcast.6) | data formatting | bytes 131072
